TPU v7x, 512 devices: a whole 4x8x8 slice. The times are simulated.
512 devices in a mesh: tm: 64 (over z, x, core), head: 8 (over y).
Axes of the slice: x: 4, y: 8, z: 8, core: 2. Of those that a mesh axis runs over, the one named last changes fastest.
Arguments:
- query_proj: bfloat16 [8192, 3072], P('tm', 'head'), may hold values from -80 to 80
- key_proj: bfloat16 [8192, 3072], P('tm', 'head'), may hold values from -80 to 80
- value_proj: bfloat16 [8192, 3072], P('tm', 'head'), may hold values from -12 to 12
- query_gain: float32 [3072], P('head'), may hold values from 0.25 to 1.75
- key_gain: float32 [3072], P('head'), may hold values from 0.25 to 1.75
- gate_table: float32 [50, 3072], P(None, 'head'), may hold values from 0.5 to 2
- frame_step: int32 [6], replicated, may hold values from 0 to 49
- far_blocks: int32 [64, 64], P('tm'), may hold values from -1 to 1, as said below
Outputs:
- attended: bfloat16 [8192, 3072], P('tm', 'head')
Inputs may be any that keep to these rules, and one draw needn't show every extreme that they name: `far_blocks`: entry [i, j] is the index of the key block of 64 tokens that query block i takes from query block j's tokens, or -1 for none; it is -1 wherever |i - j| <= 1.
All inputs are finite; a program needn't handle non-finite values.
Results may differ from a plain program's by a relative error of at most 0.007.
The roundings to bfloat16 on the way count: a program that leaves them out, or rounds other values in their place, can miss the bound.
Values may be sent and summed in bfloat16 or wider, within the bound.
A program may use at most 64 MiB of HBM per device.

v0:
```python
import jax
import jax.numpy as jnp
from jax import lax
from jax.sharding import PartitionSpec as P

HD = 128
BLK = 64
FRAME_TOK = 1560


epsilon = 1e-06


def extended(block, sides, width):
    for axis, dim in sides:
        count = lax.axis_size(axis)
        forward = [(i, i + 1) for i in range(count - 1)]
        backward = [(target, source) for source, target in forward]
        low = lax.ppermute(
            lax.slice_in_dim(block, block.shape[dim] - width, None, axis=dim), axis, forward
        )
        high = lax.ppermute(lax.slice_in_dim(block, 0, width, axis=dim), axis, backward)
        block = jnp.concatenate([low, block, high], axis=dim)
    return block


def softmax_update(carry, query_part, key_part, value_part, key_mask, score_scale):
    run_max, run_sum, accum = carry
    scores = (
        lax.dot_general(
            query_part, key_part, (((1,), (1,)), ((), ())), preferred_element_type=jnp.float32
        )
        * score_scale
    )
    scores = jnp.where(key_mask[None, :], scores, -jnp.inf)
    new_max = jnp.max(scores, axis=-1)
    fading = jnp.exp(run_max - new_max)
    weights = jnp.exp(scores - new_max[:, None])
    run_sum = run_sum * fading + jnp.sum(weights, axis=-1)
    accum = accum * fading[:, None] + jnp.dot(
        weights.astype(jnp.bfloat16), value_part, preferred_element_type=jnp.float32
    )
    return (new_max, run_sum, accum)


def local(
    query_proj, key_proj, value_proj, query_gain, key_gain, gate_table, frame_step, far_blocks
):
    row_count, feat_width = query_proj.shape
    head_count = feat_width // HD
    full_width = feat_width * lax.axis_size("head")
    query_f = query_proj.astype(jnp.float32)
    key_f = key_proj.astype(jnp.float32)
    query_sq, key_sq = lax.psum(
        (jnp.sum(query_f * query_f, axis=-1), jnp.sum(key_f * key_f, axis=-1)), "head"
    )
    query_norm = (
        query_f * lax.rsqrt(query_sq / full_width + epsilon)[:, None] * query_gain
    ).astype(jnp.bfloat16)
    key_norm = (key_f * lax.rsqrt(key_sq / full_width + epsilon)[:, None] * key_gain).astype(
        jnp.bfloat16
    )
    device_index = lax.axis_index("tm")
    device_total = lax.axis_size("tm")
    band = extended(jnp.stack([key_norm, value_proj]), (("tm", 1),), row_count)
    segment = jnp.arange(3 * row_count, dtype=jnp.int32) // row_count
    band_mask = (
        (segment == 1)
        | (segment == 0) & (device_index > 0)
        | (segment == 2) & (device_index < device_total - 1)
    )
    requests = lax.all_to_all(far_blocks, "tm", split_axis=1, concat_axis=0, tiled=True)[:, 0]
    block_count = row_count // BLK
    key_blocks = key_norm.reshape(block_count, BLK, feat_width)
    value_blocks = value_proj.reshape(block_count, BLK, feat_width)
    picked = jnp.maximum(requests, 0)
    served = (requests >= 0)[:, None, None]
    send_keys = jnp.where(served, key_blocks[picked], jnp.zeros((), jnp.bfloat16))
    send_values = jnp.where(served, value_blocks[picked], jnp.zeros((), jnp.bfloat16))
    far_keys, far_values = (
        lax.all_to_all(send_keys, "tm", split_axis=0, concat_axis=0, tiled=True),
        lax.all_to_all(send_values, "tm", split_axis=0, concat_axis=0, tiled=True),
    )
    wanted = far_blocks[0] >= 0
    positions = device_index * row_count + jnp.arange(row_count, dtype=jnp.int32)
    frame_ids = positions // FRAME_TOK
    frame_hit = frame_ids[:, None] == jnp.arange(frame_step.shape[0], dtype=jnp.int32)[None, :]
    step_rows = jnp.sum(jnp.where(frame_hit, frame_step[None, :], 0), axis=-1)
    step_hit = (
        step_rows[:, None] == jnp.arange(gate_table.shape[0], dtype=jnp.int32)[None, :]
    ).astype(jnp.float32)
    gates = jnp.dot(step_hit, gate_table, precision=lax.Precision.HIGHEST)
    score_scale = HD ** (-0.5)
    query_block = min(row_count, 512)
    far_rows = device_total * BLK
    all_keys = jnp.concatenate([band[0], far_keys.reshape(far_rows, feat_width)], axis=0)
    all_values = jnp.concatenate([band[1], far_values.reshape(far_rows, feat_width)], axis=0)
    all_mask = jnp.concatenate([band_mask, jnp.repeat(wanted, BLK)], axis=0)
    head_outputs = []
    for head_id in range(head_count):
        low = head_id * HD
        high = low + HD
        query_part = query_norm[0:query_block, low:high]
        initial = (
            jnp.full((query_block,), -jnp.inf, jnp.float32),
            jnp.zeros((query_block,), jnp.float32),
            jnp.zeros((query_block, HD), jnp.float32),
        )
        carry = softmax_update(
            initial,
            query_part,
            all_keys[:, low:high],
            all_values[:, low:high],
            all_mask,
            score_scale,
        )
        context = carry[2] / carry[1][:, None]
        row_outputs = (context * gates[0:query_block, low:high]).astype(jnp.bfloat16)
        head_outputs.append(row_outputs)
    return jnp.concatenate(head_outputs, axis=1)


def solution(mesh):
    return jax.shard_map(
        local,
        mesh=mesh,
        in_specs=(
            P("tm", "head"),
            P("tm", "head"),
            P("tm", "head"),
            P("head"),
            P("head"),
            P(None, "head"),
            P(),
            P("tm", None),
        ),
        out_specs=P("tm", "head"),
        check_vma=False,
    )
```

profile of v0, /device:TPU:7, one launch (start us, length us, event | category | flops | bytes accessed | tf_op | source)
XLA Modules:
  0.0 224.1 jit_solution(15805072511551147937)
XLA Ops:
  0.0 1.4 copy.23
  1.4 14.1 %all-to-all-start = ((s32[1,64,1]{2,0,1:T(1,128)}), s32[1,64,1]{2,0,1:T(1,128)S(1)}, u32[]{:S(2)}, u32[]{:S(2)}) async-start(s32[1,64,1]{2,0,1:T(1,128)} %copy.23), calls=%async_computation | async-start | bytes 65536 | tf_op jit(solution)/shard_map/all_to_all | solution.py:72
  15.5 1.1 fusion.80
  16.6 14.2 %all-reduce = (f32[128]{0:T(128)S(1)}, f32[128]{0:T(128)S(1)}) all-reduce(f32[128]{0:T(128)S(1)} %get-tuple-element.24, f32[128]{0:T(128)S(1)} %get-tuple-element.23), channel_id=1, replica_groups=mesh['tm'=64,'head'=8] {'head'}, use_global_device_ids=true, to_apply=%region_3.0 | all-reduce | flops 256 | bytes 2048 | tf_op jit(solution)/shard_map/psum | solution.py:54
  30.8 1.0 fusion.85
  31.7 0.0 all-to-all-done
  31.8 1.2 maximum_reduce_fusion
  33.0 0.0 copy-start.1
  33.0 2.6 %gather_fusion = bf16[64,64,384]{2,1,0:T(8,128)(2,1)} fusion(bf16[2,64,384]{2,1,0:T(8,128)(2,1)S(1)} %bitcast.18, s32[1024]{0:T(1024)S(1)} %pad_clamp_fusion), kind=kCustom, calls=%fused_computation | custom fusion | bytes 6291712 | tf_op jit(solution)/shard_map/gather | solution.py:78
  35.7 2.7 %gather_fusion.1 = bf16[64,64,384]{2,1,0:T(8,128)(2,1)} fusion(bf16[2,64,384]{2,1,0:T(8,128)(2,1)S(1)} %bitcast.15, s32[1024]{0:T(1024)S(1)} %pad_clamp_fusion), kind=kCustom, calls=%fused_computation.1 | custom fusion | bytes 6291712 | tf_op jit(solution)/shard_map/gather | solution.py:79
  38.3 1.2 compare_reduce_fusion
  39.6 4.4 %broadcast_select_fusion.1 = (bf16[64,64,384]{2,1,0:T(8,128)(2,1)S(1)}, bf16[64,64,384]{2,1,0:T(8,128)(2,1)}) fusion(bf16[64,64,384]{2,1,0:T(8,128)(2,1)S(1)} %copy-done.8, pred[64]{0:T(512)(128)(4,1)S(1)} %compare_reduce_fusion, bf16[64,64,384]{2,1,0:T(8,128)(2,1)} %gather_fusion.1), kind=kLoop, calls=%fused_computation.17 | loop fusion | flops 3145728 | bytes 12582976 | tf_op jit(solution)/shard_map/jit(_where)/select_n | solution.py:78
  44.0 85.5 %all_to_all.23 = bf16[64,64,384]{2,1,0:T(8,128)(2,1)} all-to-all(bf16[64,64,384]{2,1,0:T(8,128)(2,1)S(1)} %get-tuple-element.15), channel_id=1, replica_groups=mesh['tm'=64,'head'=8] {'tm'}, dimensions={0} | all-to-all | bytes 6291456 | tf_op jit(solution)/shard_map/all_to_all | solution.py:81
  129.6 0.0 copy-start.12
  129.6 7.6 %all-to-all-start.2 = ((bf16[64,64,384]{2,1,0:T(8,128)(2,1)}), bf16[64,64,384]{2,1,0:T(8,128)(2,1)S(1)}, u32[]{:S(2)}, u32[]{:S(2)}) async-start(bf16[64,64,384]{2,1,0:T(8,128)(2,1)} %get-tuple-element.16), calls=%async_computation.2 | async-start | bytes 6291456 | tf_op jit(solution)/shard_map/all_to_all | solution.py:82
  137.2 0.0 copy-done.9
  137.2 0.0 copy-done.11
  137.2 0.1 fusion.114
  137.3 0.7 pad_maximum_fusion.13
  138.0 2.3 %collective-permute-start.1 = (bf16[2,128,384]{2,1,0:T(8,128)(2,1)}, bf16[2,128,384]{2,1,0:T(8,128)(2,1)}, u32[]{:S(2)}, u32[]{:S(2)}) collective-permute-start(bf16[2,128,384]{2,1,0:T(8,128)(2,1)} %pad_maximum_fusion.13), channel_id=1, source_target_pairs={{8,0},{16,8},{24,16},{32,24},{40,32},{48,40},{56,48},{64,56},{72,6... | collective-permute-start | bytes 589832 | tf_op jit(solution)/shard_map/ppermute | solution.py:22
  140.3 5.4 %collective-permute-start = (bf16[2,128,384]{2,1,0:T(8,128)(2,1)}, bf16[2,128,384]{2,1,0:T(8,128)(2,1)}, u32[]{:S(2)}, u32[]{:S(2)}) collective-permute-start(bf16[2,128,384]{2,1,0:T(8,128)(2,1)} %pad_maximum_fusion.13), channel_id=1, source_target_pairs={{0,8},{8,16},{16,24},{24,32},{32,40},{40,48},{48,56},{56,64},{64,7... | collective-permute-start | bytes 589832 | tf_op jit(solution)/shard_map/ppermute | solution.py:19
  145.7 0.0 copy-done.13
  145.7 0.1 broadcast_in_dim.75
  145.8 0.1 reshape.96
  146.0 0.1 select_reduce_fusion
  146.1 1.1 fusion.86
  147.1 0.0 copy-done.12
  147.1 1.0 fusion.82
  148.1 60.9 %collective-permute-done.1 = bf16[2,128,384]{2,1,0:T(8,128)(2,1)} collective-permute-done((bf16[2,128,384]{2,1,0:T(8,128)(2,1)}, bf16[2,128,384]{2,1,0:T(8,128)(2,1)}, u32[]{:S(2)}, u32[]{:S(2)}) %collective-permute-start.1) | collective-permute-done | bytes 196640 | tf_op jit(solution)/shard_map/ppermute | solution.py:22
  209.0 0.0 collective-permute-done
  209.0 1.1 pad_maximum_fusion.12
  210.1 0.1 slice_bitcast_fusion.1
  210.2 1.9 fusion.110
  212.1 1.4 copy-done.7
  213.5 0.5 fusion.7
  214.0 0.5 fusion.111
  214.5 1.5 copy-done.5
  216.0 0.5 fusion.5
  216.5 0.6 fusion.112
  217.0 0.5 fusion.3
  217.5 0.9 exponential_multiply_fusion
  218.4 0.0 copy-done.3
  218.4 0.0 all-to-all-done.2
  218.5 2.5 %fusion.47 = bf16[128,128]{0,1:T(8,128)(2,1)S(1)} fusion(bf16[4096,384]{1,0:T(8,128)(2,1)S(1)} %bitcast.19, bf16[384,384]{1,0:T(8,128)(2,1)S(1)} %get-tuple-element.8, f32[128,4480]{1,0:T(8,128)} %copy-done.7, f32[128]{0:T(128)S(1)} %get-tuple-element.17, f32[128,384]{0,1:T(8,128)} %fusion.86, f32[128]{0:T(128)} %get-tuple-element.14, f32[128]{0:T(128)} %get-tuple-element.13), kind=kOutput, calls=%fused_computation.46 | convolution fusion | flops 150306816 | bytes 5834240 | tf_op jit(solution)/shard_map/dot_general | solution.py:40
  221.0 0.7 fusion.60
  221.7 0.9 copy-done.4
  222.6 0.7 fusion.75
  223.4 0.8 copy.27
  (30 shorter events, 0.1 us)
Async XLA Ops:
  0.0 146.1 %copy-start = (f32[50,384]{1,0:T(8,128)S(1)}, f32[50,384]{1,0:T(8,128)}, u32[]{:S(2)}) copy-start(f32[50,384]{1,0:T(8,128)} %param.13) | copy-start | bytes 230404
  1.4 30.4 %all-to-all-start = ((s32[1,64,1]{2,0,1:T(1,128)}), s32[1,64,1]{2,0,1:T(1,128)S(1)}, u32[]{:S(2)}, u32[]{:S(2)}) async-start(s32[1,64,1]{2,0,1:T(1,128)} %copy.23), calls=%async_computation | async-start | bytes 65536 | tf_op jit(solution)/shard_map/all_to_all | solution.py:72
  33.0 2.7 %copy-start.1 = (bf16[128,384]{1,0:T(8,128)(2,1)S(1)}, bf16[128,384]{1,0:T(8,128)(2,1)}, u32[]{:S(2)}) copy-start(bf16[128,384]{1,0:T(8,128)(2,1)} %param.10) | copy-start | bytes 294916
  35.6 3.9 %copy-start.8 = (bf16[64,64,384]{2,1,0:T(8,128)(2,1)S(1)}, bf16[64,64,384]{2,1,0:T(8,128)(2,1)}, u32[]{:S(2)}) copy-start(bf16[64,64,384]{2,1,0:T(8,128)(2,1)} %gather_fusion) | copy-start | bytes 9437188
  129.5 7.7 %copy-start.9 = (bf16[128,384]{1,0:T(8,128)(2,1)S(1)}, bf16[128,384]{1,0:T(8,128)(2,1)}, u32[]{:S(2)}) copy-start(bf16[128,384]{1,0:T(8,128)(2,1)} %param.9) | copy-start | bytes 294916
  129.5 7.7 %copy-start.11 = (f32[384]{0:T(512)S(1)}, f32[384]{0:T(512)}, u32[]{:S(2)}) copy-start(f32[384]{0:T(512)} %param.12) | copy-start | bytes 4612
  129.6 16.2 %copy-start.13 = (s32[1,64]{1,0:T(1,128)S(1)}, s32[1,64]{1,0:T(1,128)}, u32[]{:S(2)}) copy-start(s32[1,64]{1,0:T(1,128)} %param.15) | copy-start | bytes 772
  129.6 16.4 %copy-start.14 = (s32[6]{0:T(128)S(1)}, s32[6]{0:T(128)}, u32[]{:S(2)}) copy-start(s32[6]{0:T(128)} %param.14) | copy-start | bytes 76
  129.6 17.6 %copy-start.12 = (f32[384]{0:T(512)S(1)}, f32[384]{0:T(512)}, u32[]{:S(2)}) copy-start(f32[384]{0:T(512)} %param.11) | copy-start | bytes 4612
  129.6 88.9 %all-to-all-start.2 = ((bf16[64,64,384]{2,1,0:T(8,128)(2,1)}), bf16[64,64,384]{2,1,0:T(8,128)(2,1)S(1)}, u32[]{:S(2)}, u32[]{:S(2)}) async-start(bf16[64,64,384]{2,1,0:T(8,128)(2,1)} %get-tuple-element.16), calls=%async_computation.2 | async-start | bytes 6291456 | tf_op jit(solution)/shard_map/all_to_all | solution.py:82
  138.0 71.0 %collective-permute-start.1 = (bf16[2,128,384]{2,1,0:T(8,128)(2,1)}, bf16[2,128,384]{2,1,0:T(8,128)(2,1)}, u32[]{:S(2)}, u32[]{:S(2)}) collective-permute-start(bf16[2,128,384]{2,1,0:T(8,128)(2,1)} %pad_maximum_fusion.13), channel_id=1, source_target_pairs={{8,0},{16,8},{24,16},{32,24},{40,32},{48,40},{56,48},{64,56},{72,6... | collective-permute-start | bytes 589832 | tf_op jit(solution)/shard_map/ppermute | solution.py:22
  140.3 68.7 %collective-permute-start = (bf16[2,128,384]{2,1,0:T(8,128)(2,1)}, bf16[2,128,384]{2,1,0:T(8,128)(2,1)}, u32[]{:S(2)}, u32[]{:S(2)}) collective-permute-start(bf16[2,128,384]{2,1,0:T(8,128)(2,1)} %pad_maximum_fusion.13), channel_id=1, source_target_pairs={{0,8},{8,16},{16,24},{24,32},{32,40},{40,48},{48,56},{56,64},{64,7... | collective-permute-start | bytes 589832 | tf_op jit(solution)/shard_map/ppermute | solution.py:19
  210.2 3.8 %copy-start.2 = (bf16[64,64,384]{2,1,0:T(8,128)(2,1)S(1)}, bf16[64,64,384]{2,1,0:T(8,128)(2,1)}, u32[]{:S(2)}) copy-start(bf16[64,64,384]{2,1,0:T(8,128)(2,1)} %all_to_all.23) | copy-start | bytes 9437188
  212.1 1.4 copy-start.7
  214.5 1.5 copy-start.5
  217.0 1.4 copy-start.3
  218.4 2.5 %copy-start.6 = (f32[128,4480]{1,0:T(8,128)S(1)}, f32[128,4480]{1,0:T(8,128)}, u32[]{:S(2)}) copy-start(f32[128,4480]{1,0:T(8,128)} %copy-done.5) | copy-start | bytes 6881284
  218.4 2.5 %copy-start.10 = (f32[128,384]{0,1:T(8,128)S(1)}, f32[128,384]{0,1:T(8,128)}, u32[]{:S(2)}) copy-start(f32[128,384]{0,1:T(8,128)} %fusion.86) | copy-start | bytes 589828
  221.0 1.6 copy-start.4
where the time goes:
time: 225 us; the launch traced here: 224 us
  blocking collectives  99.7 us (44%)
  waiting for transfers between devices  60.9 us (27%)
  starting transfers between devices  29.4 us (13%)
  other arithmetic  14.2 us (6%)
  local copies, waits for them, and re-layouts  11.6 us (5%)
  matrix products  8.01 us (4%)
    all_to_all x1, blocking collectives, local(): lax.all_to_all(send_keys, 'tm', split_axis=0, concat_axis=0, tiled=True)  85.5 us
    ppermute x1, waiting for transfers between devices, extended(): lax.ppermute(lax.slice_in_dim(block, 0, width, axis=dim), axis, backward)  60.9 us
    psum x1, blocking collectives, local(): lax.psum((jnp.sum(query_f * query_f, axis=-1), jnp.sum(key_f * key_f, axi...  14.2 us
    all_to_all x1, starting transfers between devices, local(): lax.all_to_all(far_blocks, 'tm', split_axis=1, concat_axis=0, tiled=True)  14.1 us
    all_to_all x1, starting transfers between devices, local(): lax.all_to_all(send_values, 'tm', split_axis=0, concat_axis=0, tiled=True)  7.64 us
    ppermute x1, starting transfers between devices, extended(): lax.ppermute(lax.slice_in_dim(block, block.shape[dim] - width, None, axis...  5.4 us
  transfers between devices with their start and end apart: 4, of which 1 were waited for; matrix products, arithmetic and copies ran while one was open for 5% of the time, Pallas kernels for 0%

commit v1 on v0

v1 whole, which is shorter than its diff:
```python
import functools

import jax
import jax.numpy as jnp
from jax import lax
from jax.experimental import pallas as pl
from jax.experimental.pallas import tpu as pltpu
from jax.sharding import PartitionSpec as P

HD = 128
TOK = 128
BLK = 64
FRAME_TOK = 1560
NZ, NX, NC = 8, 4, 2
NH = 3
EPS = 1e-06
MASKED = -1e30
GROUP = 4
LOG2E = 1.4426950408889634
COEF = HD**-0.5 * LOG2E
MESH = pl.DeviceIdType.MESH
BF16 = jnp.bfloat16
F32 = jnp.float32


def kernel(
    ny,
    q_hbm, k_hbm, v_hbm, qg_hbm, kg_hbm, gate_hbm, frame_ref, far_ref,
    out_ref,
    qin, kin, qg_in, kg_in, gate_in, qst,
    v_own, v_left, v_right, v_far, k_own, k_left, k_right, k_far, k_raw, isc, inv_buf, qbuf, fst, fbuf, fsm, sst, sbuf, bias,
    m_ref, l_ref, acc_ref, ost, stst, obuf, stb,
    load_sem, own_sem, fsm_sem,
    s_send, s_recv, f_send, f_recv, q_send, q_recv,
    p1_send, p1_recv, i_send, i_recv, x_send, x_recv, c_send, c_recv,
    o_send, o_recv, t_send, t_recv,
):
    tm = lax.axis_index("tm")
    y = lax.axis_index("head")
    c = lax.rem(tm, NC)
    x = lax.rem(tm // NC, NX)
    z = tm // (NC * NX)
    head = lax.rem(z, 4)
    active = head < NH
    xl, xr = lax.rem(x + 3, NX), lax.rem(x + 1, NX)
    colx = (x, xl, xr, lax.rem(x + 2, NX))

    def dev(zz, xx, cc):
        return (zz * (NX * NC) + xx * NC + cc, y)

    def remote(src, dst, ss, rs, target):
        return pltpu.make_async_remote_copy(
            src_ref=src, dst_ref=dst, send_sem=ss, recv_sem=rs,
            device_id=target, device_id_type=MESH,
        )

    loads = [
        pltpu.make_async_copy(s, d, load_sem.at[i])
        for i, (s, d) in enumerate(((k_hbm, kin), (q_hbm, qin)))
    ]
    late_loads = [
        pltpu.make_async_copy(s, d, load_sem.at[2 + i])
        for i, (s, d) in enumerate(((qg_hbm, qg_in), (kg_hbm, kg_in), (gate_hbm, gate_in)))
    ]
    for cp in loads + late_loads:
        cp.start()

    barrier = pltpu.get_barrier_semaphore()
    partners = [(tm, lax.rem(y + d, ny)) for d in range(1, ny)]
    partners += [dev(lax.rem(z + d, NZ), x, c) for d in range(1, NZ)]
    partners += [dev(z, xl, c), dev(z, xr, c), dev(z, x, 1 - c)]
    for p in partners:
        pl.semaphore_signal(barrier, inc=1, device_id=p, device_id_type=MESH)

    for cp in loads:
        cp.wait()

    def square_sums(ref):
        f = ref[...].astype(F32)
        sq = f * f
        part = sq[:, 0:HD] + sq[:, HD : 2 * HD] + sq[:, 2 * HD : 3 * HD]
        return jnp.sum(part.T, axis=0, keepdims=True)

    sst[...] = jnp.concatenate(
        [square_sums(qin), square_sums(kin), jnp.zeros((6, TOK), F32)], axis=0
    )
    sbuf[y] = sst[...]
    far_row = jnp.concatenate([far_ref[...], jnp.full((1, 64), -1, jnp.int32)], axis=1)
    fst[...] = jnp.broadcast_to(far_row, (8, 128))

    pl.semaphore_wait(barrier, len(partners))

    s_copies = []
    for d in range(1, ny):
        cp = remote(sst, sbuf.at[y], s_send.at[d - 1], s_recv.at[d - 1], (tm, lax.rem(y + d, ny)))
        cp.start()
        s_copies.append(cp)

    place = []
    for h in range(NH):
        k = lax.rem(z - h + 1 + NZ, NZ)
        place.append((h + 4 * (k // 4), lax.rem(k, 4)))

    def row_copies(t, h):
        row, slot = place[h]
        cols = pl.ds(h * HD, HD)
        if t == 1:
            ends = [(k_hbm.at[:, cols], k_raw.at[slot])]
        else:
            ends = [(v_hbm.at[pl.ds(p * BLK, BLK), cols], v_own.at[c, slot, p]) for p in range(2)]
        return [
            remote(src, dst, p1_send.at[t + p, h], p1_recv.at[t, slot], dev(row, x, c))
            for p, (src, dst) in zip((0, 2), ends)
        ]

    def inv_copy(h):
        row, slot = place[h]
        return remote(isc, inv_buf.at[slot], i_send.at[h], i_recv.at[slot], dev(row, x, c))

    def own_copies(t, h):
        cols = pl.ds(h * HD, HD)
        if t == 1:
            return [pltpu.make_async_copy(k_hbm.at[:, cols], k_raw.at[1], own_sem.at[2])]
        return [
            pltpu.make_async_copy(
                v_hbm.at[pl.ds(p * BLK, BLK), cols], v_own.at[c, 1, p], own_sem.at[p]
            )
            for p in range(2)
        ]

    def to_rows(t):
        for h, (row, _) in enumerate(place):

            @pl.when(row != z)
            def _():
                for cp in row_copies(t, h):
                    cp.start()

            @pl.when(row == z)
            def _():
                for cp in own_copies(t, h):
                    cp.start()

    def row_arrived(t, slot):
        if slot == 1:
            for cp in own_copies(t, 0):
                cp.wait()
        else:
            ref = k_raw.at[slot] if t == 1 else v_own.at[c, slot]
            remote(
                ref, ref, p1_send.at[t, 0], p1_recv.at[t, slot], dev(z, x, 1 - c)
            ).wait_recv()

    bufs = ((v_own, v_left, v_right, v_far), (k_own, k_left, k_right, k_far))

    def x_copy(t, lane, item):
        if item < 2:
            here, there, half = 0, 1 + lane, item
        else:
            here, there, half = 1 + lane, 3, lane
        part = pl.ds(2 * half, 2)
        return remote(
            bufs[t][here].at[c, part], bufs[t][there].at[c, part],
            x_send.at[t, lane, item], x_recv.at[t, lane, item],
            dev(z, xr if lane == 0 else xl, c),
        )

    def x_arrived(t, lane, item):
        x_copy(t, lane, item).wait_recv()

    def c_copy(t, col, half):
        ref = bufs[t][col].at[c, pl.ds(2 * half, 2)]
        return remote(
            ref, ref, c_send.at[t, col, half], c_recv.at[t, col, half], dev(z, x, 1 - c)
        )

    def c_arrived(t, col):
        for half in range(2):
            ref = bufs[t][col].at[1 - c, pl.ds(2 * half, 2)]
            remote(
                ref, ref, c_send.at[t, col, half], c_recv.at[t, col, half], dev(z, x, 1 - c)
            ).wait_recv()

    def key_ready(slot):
        row_arrived(1, slot)
        if slot != 1:
            remote(
                isc, inv_buf.at[slot], i_send.at[0], i_recv.at[slot], dev(z, x, 1 - c)
            ).wait_recv()
        scale = jnp.broadcast_to(inv_buf[slot][1:2, :], (TOK, HD)).T
        gain = kg_in[pl.ds(pl.multiple_of(head * HD, HD), HD)].reshape(1, HD)
        keys = (k_raw[slot].astype(F32) * scale * gain).astype(BF16)
        k_own[c, slot] = keys.reshape(2, BLK, HD)

    def spread_own(t):
        ready = key_ready if t == 1 else functools.partial(row_arrived, 0)
        ready(1)
        ready(0)
        x_copy(t, 0, 0).start()
        c_copy(t, 0, 0).start()
        ready(2)
        ready(3)
        x_copy(t, 1, 1).start()
        x_copy(t, 0, 1).start()
        x_copy(t, 1, 0).start()
        c_copy(t, 0, 1).start()

    def relay(t):
        x_arrived(t, 0, 0)
        x_copy(t, 0, 2).start()
        c_copy(t, 1, 0).start()
        x_arrived(t, 1, 1)
        x_copy(t, 1, 2).start()
        c_copy(t, 2, 1).start()

    def rest(t):
        x_arrived(t, 0, 1)
        c_copy(t, 1, 1).start()
        x_arrived(t, 1, 0)
        c_copy(t, 2, 0).start()

    def opposite(t):
        x_arrived(t, 0, 2)
        c_copy(t, 3, 0).start()
        x_arrived(t, 1, 2)
        c_copy(t, 3, 1).start()

    to_rows(0)
    to_rows(1)

    rows = [(h, part) for h in range(NH) for part in range(2)]

    def f_copy(i):
        h, part = rows[i]
        return remote(fst, fbuf.at[z], f_send.at[i], f_recv.at[z], dev(h + 4 * part, x, c))

    def q_copy(i):
        h, part = rows[i]
        return remote(qst.at[h], qbuf.at[z], q_send.at[i], q_recv.at[z], dev(h + 4 * part, x, c))

    for i, (h, part) in enumerate(rows):

        @pl.when(h + 4 * part != z)
        def _():
            f_copy(i).start()

    fbuf[z] = fst[...]

    @pl.when(active)
    def _():
        spread_own(0)

    for cp in s_copies:
        cp.wait()
    totals = sbuf[0]
    for i in range(1, ny):
        totals = totals + sbuf[i]
    for cp in late_loads:
        cp.wait()
    inv = lax.rsqrt(totals / (NH * HD * ny) + EPS)

    def normed(ref, row, gain_ref, h):
        span = slice(h * HD, (h + 1) * HD)
        scale = jnp.broadcast_to(inv[row : row + 1, :], (TOK, HD)).T
        return (ref[:, span].astype(F32) * scale * gain_ref[span].reshape(1, HD)).astype(BF16)

    isc[...] = inv
    inv_buf[1] = inv
    for h, (row, _) in enumerate(place):

        @pl.when(row != z)
        def _():
            inv_copy(h).start()

    for h in range(NH):
        qst[h] = normed(qin, 0, qg_in, h)
    for i, (h, part) in enumerate(rows):

        @pl.when(h + 4 * part != z)
        def _():
            q_copy(i).start()

        @pl.when(h + 4 * part == z)
        def _():
            qbuf[z] = qst[h]

    lane = lax.broadcasted_iota(jnp.int32, (1, HD), 1)
    lane_sq = lax.broadcasted_iota(jnp.int32, (TOK, HD), 1)

    def o_copy(zz):
        return remote(
            ost.at[zz], obuf.at[head, z // 4], o_send.at[zz], o_recv.at[head, z // 4], dev(zz, x, c)
        )

    def t_copy(zz):
        return remote(
            stst.at[zz], stb.at[head, z // 4], t_send.at[zz], t_recv.at[head, z // 4], dev(zz, x, c)
        )

    def band_slot(zz, d):
        j = zz * 8 + x * 2 + c + d
        zj = jnp.clip(j, 0, 63) // 8
        slot = lax.rem(zj - z + 1 + NZ, NZ)
        ok = (slot < 4) & (j >= 0) & (j <= 63)
        return jnp.minimum(slot, 3), jnp.where(ok, 0.0, MASKED).astype(F32)

    def half(ref, core, slot, pick):
        return ref[core, slot, pick]

    def attend(col, zz):
        key_parts, value_parts = [], []
        keys_of, values_of = bufs[1][col], bufs[0][col]
        for core in range(NC):
            for slot in range(4):
                owner = lax.rem(z - 1 + slot + NZ, NZ) * 8 + colx[col] * 2 + core
                pick = jnp.maximum(fsm[zz, 0, owner], 0)
                key_parts.append(half(keys_of, core, slot, pick))
                value_parts.append(half(values_of, core, slot, pick))
        add = [bias[col, pl.ds(zz, 1), :]]
        if col == 0:
            slot, own = band_slot(zz, 0)
            slot_two, two = band_slot(zz, 1 - 2 * c)
            for core, at in ((c, slot), (1 - c, slot_two)):
                key_parts.append(half(keys_of, core, at, 1))
                value_parts.append(half(values_of, core, at, 1))
            add.append(jnp.where(lane < BLK, own, two))
        if col == 3:
            slot, ok = band_slot(zz, 2 * c - 1)
            for of, parts in ((bufs[1], key_parts), (bufs[0], value_parts)):
                part = jnp.where(c == 0, half(of[1], 1, slot, 1), half(of[2], 0, slot, 1))
                parts += [part, part]
            add.append(jnp.where(lane < BLK, ok, MASKED))
        keys = jnp.concatenate(key_parts, axis=0)
        values = jnp.concatenate(value_parts, axis=0)
        scores = lax.dot_general(
            qbuf[zz], keys, (((1,), (1,)), ((), ())), preferred_element_type=F32
        ) + jnp.concatenate(add, axis=1)
        return [scores[:, i * HD : (i + 1) * HD] for i in range(scores.shape[1] // HD)], values

    def chunk_steps(col, blocks):
        first, last = col == 0, col == 3
        scored = [attend(col, zz) for zz in blocks]
        tops, fades, totals_of, contexts = [], [], [], []
        for zz, (tiles, _) in zip(blocks, scored):
            top = functools.reduce(jnp.maximum, tiles)
            top = jnp.broadcast_to(jnp.max(top, axis=1, keepdims=True), (TOK, HD))
            if not first:
                old = m_ref[zz]
                top = jnp.maximum(old, top)
                fades.append(jnp.exp2((old - top) * COEF))
            tops.append(top)
        for i, (zz, (tiles, values)) in enumerate(zip(blocks, scored)):
            tiles = [jnp.exp2((t - tops[i]) * COEF) for t in tiles]
            total = functools.reduce(jnp.add, tiles)
            weights = jnp.concatenate([t.astype(BF16) for t in tiles], axis=1)
            context = jnp.dot(weights, values, preferred_element_type=F32)
            if not first:
                total = l_ref[zz] * fades[i] + total
                context = acc_ref[zz] * fades[i] + context
            totals_of.append(total)
            contexts.append(context)
        if not last:
            for zz, top, total, context in zip(blocks, tops, totals_of, contexts):
                m_ref[zz] = top
                l_ref[zz] = total
                acc_ref[zz] = context
            return
        results = []
        for top, total, context in zip(tops, totals_of, contexts):
            total = jnp.broadcast_to(jnp.sum(total, axis=1, keepdims=True), (TOK, HD))
            stats = jnp.where(lane_sq == 0, top, total).T[0:8]
            results.append(((context / total).astype(BF16), stats))
        for zz, (context, stats) in zip(blocks, results):
            ost[zz] = context
            stst[zz] = stats
        for zz, (context, stats) in zip(blocks, results):

            @pl.when(zz == z)
            def _():
                obuf[head, z // 4] = context
                stb[head, z // 4] = stats

            @pl.when(zz != z)
            def _():
                o_copy(zz).start()
                t_copy(zz).start()

    def chunk(col):
        def body(i, carry):
            blocks = []
            for j in range(GROUP):
                k = (GROUP // 2) * i + (j + 1) // 2
                blocks.append(lax.rem(z + 4 + (k if j % 2 == 0 else -k) + NZ, NZ))
            chunk_steps(col, blocks)
            return carry

        lax.fori_loop(0, NZ // GROUP, body, 0)

    @pl.when(active)
    def _():
        for d in range(1, NZ):
            zz = lax.rem(z + d, NZ)
            remote(fst, fbuf.at[zz], f_send.at[0], f_recv.at[zz], dev(zz, x, c)).wait_recv()
        cp = pltpu.make_async_copy(fbuf, fsm, fsm_sem)
        cp.start()
        relay(0)
        spread_own(1)
        far = fbuf[:, 0, 0:64]
        block = lax.broadcasted_iota(jnp.int32, (NZ, 64), 0) * 8 + x * 2 + c
        other = lax.broadcasted_iota(jnp.int32, (NZ, 64), 1)
        valid = jnp.where((far >= 0) | (jnp.abs(block - other) <= 1), 1.0, 0.0).astype(BF16)
        at = lax.broadcasted_iota(jnp.int32, (64, 512), 1) // BLK
        src = lax.broadcasted_iota(jnp.int32, (64, 512), 0)
        zsrc = lax.rem(z - 1 + lax.rem(at, 4) + NZ, NZ)
        for col in range(NX):
            spread = (src == zsrc * 8 + colx[col] * 2 + at // 4).astype(F32).astype(BF16)
            hit = jnp.dot(valid, spread, preferred_element_type=F32)
            bias[col] = jnp.where(hit > 0.5, 0.0, MASKED)
        rest(0)
        opposite(0)
        cp.wait()
        relay(1)
        for d in range(1, NZ):
            zz = lax.rem(z + d, NZ)
            remote(qst.at[0], qbuf.at[zz], q_send.at[0], q_recv.at[zz], dev(zz, x, c)).wait_recv()
        c_arrived(0, 0)
        c_arrived(1, 0)
        chunk(0)
        rest(1)
        c_arrived(0, 1)
        c_arrived(1, 1)
        chunk(1)
        opposite(1)
        c_arrived(0, 2)
        c_arrived(1, 2)
        chunk(2)
        c_arrived(0, 3)
        c_arrived(1, 3)
        chunk(3)

    start = tm * TOK
    frame = start // FRAME_TOK
    after = jnp.minimum(frame + 1, 5)
    steps = lax.broadcasted_iota(jnp.int32, gate_in.shape, 0)

    def gate_of(step):
        return jnp.sum(jnp.where(steps == step, gate_in[...], 0.0), axis=0, keepdims=True)

    gate_a, gate_b = gate_of(frame_ref[frame]), gate_of(frame_ref[after])
    edge = (frame + 1) * FRAME_TOK - start
    before = lax.broadcasted_iota(jnp.int32, (TOK, HD), 0) < edge
    for h in range(NH):
        for part in range(2):

            @pl.when(h + 4 * part != z)
            def _():
                remote(
                    ost.at[0], obuf.at[h, part], o_send.at[0], o_recv.at[h, part], dev(z, x, 1 - c)
                ).wait_recv()
                remote(
                    stst.at[0], stb.at[h, part], t_send.at[0], t_recv.at[h, part], dev(z, x, 1 - c)
                ).wait_recv()

        span = slice(h * HD, (h + 1) * HD)
        one, two = stb[h, 0], stb[h, 1]
        top = jnp.maximum(one[0:1], two[0:1])
        weight_one = one[1:2] * jnp.exp2((one[0:1] - top) * COEF)
        weight_two = two[1:2] * jnp.exp2((two[0:1] - top) * COEF)
        share = weight_one / (weight_one + weight_two)
        share = jnp.broadcast_to(share, (TOK, HD)).T
        context = obuf[h, 0].astype(F32) * share + obuf[h, 1].astype(F32) * (1.0 - share)
        gate = jnp.where(before, gate_a[:, span], gate_b[:, span])
        out_ref[:, span] = (context * gate).astype(BF16)

    for h, (row, _) in enumerate(place):

        @pl.when(row != z)
        def _():
            for cp in row_copies(0, h) + row_copies(1, h):
                cp.wait_send()
            inv_copy(h).wait_send()

    for i, (h, part) in enumerate(rows):

        @pl.when(h + 4 * part != z)
        def _():
            f_copy(i).wait_send()
            q_copy(i).wait_send()

    @pl.when(active)
    def _():
        for t in range(2):
            for ln in range(2):
                for item in range(3):
                    x_copy(t, ln, item).wait_send()
            for col in range(4):
                for half in range(2):
                    c_copy(t, col, half).wait_send()
        for d in range(1, NZ):
            zz = lax.rem(z + d, NZ)
            o_copy(zz).wait_send()
            t_copy(zz).wait_send()


def solution(mesh):
    ny = mesh.shape["head"]
    dma = pltpu.SemaphoreType.DMA
    vmem = pltpu.VMEM

    def local(query, key, value, query_gain, key_gain, gate_table, frame_step, far_blocks):
        whole = pl.BlockSpec(memory_space=pltpu.VMEM)
        hbm = pl.BlockSpec(memory_space=pltpu.HBM)
        width = NH * HD
        return pl.pallas_call(
            functools.partial(kernel, ny),
            out_shape=jax.ShapeDtypeStruct((TOK, width), BF16),
            in_specs=[hbm] * 6 + [pl.BlockSpec(memory_space=pltpu.SMEM), whole],
            out_specs=whole,
            scratch_shapes=[
                vmem((TOK, width), BF16),
                vmem((TOK, width), BF16),
                vmem((width,), F32),
                vmem((width,), F32),
                vmem((50, width), F32),
                vmem((NH, TOK, HD), BF16),
                *[vmem((NC, 4, 2, BLK, HD), BF16)] * 8,
                vmem((4, TOK, HD), BF16),
                vmem((8, TOK), F32),
                vmem((4, 8, TOK), F32),
                vmem((NZ, TOK, HD), BF16),
                vmem((8, 128), jnp.int32),
                vmem((NZ, 8, 128), jnp.int32),
                pltpu.SMEM((NZ, 8, 128), jnp.int32),
                vmem((8, TOK), F32),
                vmem((ny, 8, TOK), F32),
                vmem((NX, NZ, 512), F32),
                vmem((NZ, TOK, HD), F32),
                vmem((NZ, TOK, HD), F32),
                vmem((NZ, TOK, HD), F32),
                vmem((NZ, TOK, HD), BF16),
                vmem((NZ, 8, TOK), F32),
                vmem((NH, 2, TOK, HD), BF16),
                vmem((NH, 2, 8, TOK), F32),
                dma((5,)), dma((3,)), dma,
                dma((ny,)), dma((ny,)), dma((6,)), dma((NZ,)), dma((6,)), dma((NZ,)),
                dma((3, 3)), dma((2, 4)), dma((3,)), dma((4,)), dma((2, 2, 3)), dma((2, 2, 3)),
                dma((2, 4, 2)), dma((2, 4, 2)),
                dma((NZ,)), dma((NH, 2)), dma((NZ,)), dma((NH, 2)),
            ],
            compiler_params=pltpu.CompilerParams(
                collective_id=0, has_side_effects=True, vmem_limit_bytes=56 * 2**20
            ),
            name="attend",
        )(
            query, key, value, query_gain, key_gain,
            gate_table, frame_step, far_blocks,
        )

    return jax.shard_map(
        local,
        mesh=mesh,
        in_specs=(
            P("tm", "head"),
            P("tm", "head"),
            P("tm", "head"),
            P("head"),
            P("head"),
            P(None, "head"),
            P(),
            P("tm", None),
        ),
        out_specs=P("tm", "head"),
        check_vma=False,
    )
```

time: 225 us -> 47.8 us (0.21)
  the two profiles are of different devices: /device:TPU:7 before, /device:TPU:1 now
where the time goes in v1:
time: 47.8 us; the launch traced here: 47.5 us
  Pallas kernels  46 us (96%)
  local copies, waits for them, and re-layouts  1.54 us (3%)
    pallas_call x1, Pallas kernels, local(): pl.pallas_call(functools.partial(kernel, ny), out_shape=jax.ShapeDtypeStr...  46 us
    unnamed x1, local copies, waits for them, and re-layouts  1.54 us

profile of v1, /device:TPU:1, one launch (start us, length us, event | category | flops | bytes accessed | tf_op | source)
XLA Modules:
  0.0 47.5 jit_solution(5250682777072739979)
XLA Ops:
  0.0 46.0 %attend.1 = bf16[128,384]{1,0:T(8,128)(2,1)} custom-call(bf16[128,384]{1,0:T(8,128)(2,1)} %q_hbm.1, bf16[128,384]{1,0:T(8,128)(2,1)} %k_hbm.1, bf16[128,384]{1,0:T(8,128)(2,1)} %v_hbm.1, f32[384]{0:T(512)} %qg_hbm.1, f32[384]{0:T(512)} %kg_hbm.1, f32[50,384]{1,0:T(8,128)} %gate_hbm.1, s32[6]{0:T(128)} %frame_ref.1, s32[1,64]{1,0:T(1,128)} %far_ref.1), custom_call_target="tpu_custom_call" | custom-call | tf_op jit(solution)/shard_map/attend/pallas_call | solution.py:514
  46.0 1.5 %copy.10 = bf16[128,384]{1,0:T(8,128)(2,1)} copy(bf16[128,384]{1,0:T(8,128)(2,1)} %attend.1) | data formatting | bytes 196608

commit v2 on v1

v2 whole, which is shorter than its diff:
```python
import functools

import jax
import jax.numpy as jnp
from jax import lax
from jax.experimental import pallas as pl
from jax.experimental.pallas import tpu as pltpu
from jax.sharding import PartitionSpec as P

HD = 128
TOK = 128
BLK = 64
FRAME_TOK = 1560
NZ, NX, NC = 8, 4, 2
NH = 3
EPS = 1e-06
MASKED = -1e30
GROUP = 4
LOG2E = 1.4426950408889634
COEF = HD**-0.5 * LOG2E
MESH = pl.DeviceIdType.MESH
BF16 = jnp.bfloat16
F32 = jnp.float32

ROWS = (0, 1, 2, 4, 5, 6)


def kernel(
    ny,
    q_hbm, k_hbm, v_hbm, qg_hbm, kg_hbm, gate_hbm, frame_ref, far_ref,
    out_ref,
    qin, kin, qg_in, kg_in, gate_in, q_raw, k_raw, v_raw, isc, inv_own, inv_buf, qbuf,
    fst, fbuf, fsm, sst, sbuf, bias, m_ref, l_ref, acc_ref, ost, stst, obuf, stb,
    *rest,
):
    keys_at, values_at = (rest[0:4], rest[4:8]), (rest[8:12], rest[12:16])
    (
        load_sem, own_sem, fsm_sem, hello, hello_y,
        s_send, s_recv, f_send, f_recv, q_send, q_recv,
        p1_send, p1_recv, io_send, io_recv, i_send, i_recv, x_send, x_recv, c_send, c_recv,
        o_send, o_recv, t_send, t_recv,
    ) = rest[16:]
    tm = lax.axis_index("tm")
    y = lax.axis_index("head")
    c = lax.rem(tm, NC)
    x = lax.rem(tm // NC, NX)
    z = tm // (NC * NX)
    part, slot_mine = z // 4, lax.rem(z, 4)
    active = slot_mine < 3
    head = jnp.minimum(slot_mine, 2)
    xl, xr = lax.rem(x + 3, NX), lax.rem(x + 1, NX)
    colx = (x, xl, xr, lax.rem(x + 2, NX))

    def dev(zz, xx, cc):
        return (zz * (NX * NC) + xx * NC + cc, y)

    def remote(src, dst, ss, rs, target):
        return pltpu.make_async_remote_copy(
            src_ref=src, dst_ref=dst, send_sem=ss, recv_sem=rs,
            device_id=target, device_id_type=MESH,
        )

    loads = [
        pltpu.make_async_copy(s, d, load_sem.at[i])
        for i, (s, d) in enumerate(((k_hbm, kin), (q_hbm, qin)))
    ]
    late_loads = [
        pltpu.make_async_copy(s, d, load_sem.at[2 + i])
        for i, (s, d) in enumerate(((qg_hbm, qg_in), (kg_hbm, kg_in), (gate_hbm, gate_in)))
    ]
    for cp in loads + late_loads:
        cp.start()

    barrier = pltpu.get_barrier_semaphore()

    def greet(target):
        pl.semaphore_signal(barrier, inc=1, device_id=target, device_id_type=MESH)

    for d in range(1, NX):
        greet(dev(z, lax.rem(x + d, NX), c))
    greet(dev(z, x, 1 - c))
    for yy in range(1, ny):

        @pl.when(yy > y)
        def _():
            greet((tm, yy))

    for zz in range(1, NZ):

        @pl.when(zz > z)
        def _():
            greet(dev(zz, x, c))

        @pl.when((zz > z) & (zz // 4 == part))
        def _():
            for d in range(1, NX):
                greet(dev(zz, lax.rem(x + d, NX), c))

    pl.semaphore_wait(barrier, NX + z + 3 * slot_mine + y)

    for zz in range(NZ - 1):

        @pl.when(active & (zz < z))
        def _():
            pl.semaphore_signal(hello.at[z], inc=1, device_id=dev(zz, x, c), device_id_type=MESH)

    for yy in range(ny - 1):

        @pl.when(yy < y)
        def _():
            pl.semaphore_signal(hello_y.at[y], inc=1, device_id=(tm, yy), device_id_type=MESH)

    def await_row(row):
        @pl.when(row > z)
        def _():
            pl.semaphore_wait(hello.at[row], 1)

    def row_copies(h):
        row, cols = h + 4 * part, pl.ds(h * HD, HD)
        return [
            remote(
                ref.at[:, cols], dst, p1_send.at[t, h], p1_recv.at[t, slot_mine], dev(row, x, c)
            )
            for t, (ref, dst) in enumerate(
                ((v_hbm, v_raw.at[slot_mine]), (k_hbm, k_raw.at[0, slot_mine]))
            )
        ]

    def own_copy(t, h):
        ref, dst = (
            (v_hbm, v_raw.at[slot_mine]), (k_hbm, k_raw.at[0, slot_mine]), (q_hbm, q_raw.at[z])
        )[t]
        return pltpu.make_async_copy(ref.at[:, pl.ds(h * HD, HD)], dst, own_sem.at[t])

    def f_copy(i):
        return remote(fst, fbuf.at[z], f_send.at[i], f_recv.at[z], dev(ROWS[i], x, c))

    def q_copy(i):
        source = q_hbm.at[:, pl.ds(i % NH * HD, HD)]
        return remote(source, q_raw.at[z], q_send.at[i], q_recv.at[z], dev(ROWS[i], x, c))

    def queries_to(i):
        @pl.when(ROWS[i] != z)
        def _():
            f_copy(i).start()
            q_copy(i).start()

    far_row = jnp.concatenate([far_ref[...], jnp.full((1, 64), -1, jnp.int32)], axis=1)
    fst[...] = jnp.broadcast_to(far_row, (8, 128))
    fbuf[z] = fst[...]
    for p in range(2):

        @pl.when(part == p)
        def _():
            for h in range(NH):
                row = h + 4 * p
                await_row(row)

                @pl.when(row != z)
                def _():
                    for cp in row_copies(h):
                        cp.start()

                @pl.when(row == z)
                def _():
                    for t in range(3):
                        own_copy(t, h).start()

    for cp in loads:
        cp.wait()

    def square_sums(ref):
        f = ref[...].astype(F32)
        sq = f * f
        sq = sq[:, 0:HD] + sq[:, HD : 2 * HD] + sq[:, 2 * HD : 3 * HD]
        return jnp.sum(sq.T, axis=0, keepdims=True)

    sst[...] = jnp.concatenate(
        [square_sums(qin), square_sums(kin), jnp.zeros((6, TOK), F32)], axis=0
    )
    sbuf[y] = sst[...]

    def s_copy(yy):
        return remote(sst, sbuf.at[y], s_send.at[yy], s_recv.at[y], (tm, yy))

    for yy in range(ny - 1):

        @pl.when(yy < y)
        def _():
            s_copy(yy).start()

    @pl.when(part == 0)
    def _():
        for i in range(3):
            queries_to(i)

    for yy in range(1, ny):

        @pl.when(yy > y)
        def _():
            pl.semaphore_wait(hello_y.at[yy], 1)
            s_copy(yy).start()

    def arrived(ref, sem):
        remote(ref, ref, s_send.at[0], sem, dev(z, x, 1 - c)).wait_recv()

    def row_arrived(t, slot):
        ref = (v_raw.at[slot], k_raw.at[0, slot])[t]

        @pl.when(slot == slot_mine)
        def _():
            own_copy(t, 0).wait()

        @pl.when(slot != slot_mine)
        def _():
            arrived(ref, p1_recv.at[t, slot])

    def k_half(col, half):
        return k_raw.at[col, pl.ds(2 * half, 2)]

    def x_copy(t, lane, half):
        if t == 1:
            src, dst = k_half(0, half), k_half(1 + lane, half)
        else:
            src, dst = values_at[half][0].at[c], values_at[half][1 + lane].at[c]
        return remote(
            src, dst, x_send.at[t, lane, half], x_recv.at[t, lane, half],
            dev(z, lax.rem(x + (1, 3, 2)[lane], NX), c),
        )

    def x_arrived(t, lane, half):
        x_copy(t, lane, half).wait_recv()

    def c_copy(t, col, half):
        ref = (values_at, keys_at)[t][half][col].at[c]
        return remote(
            ref, ref, c_send.at[t, col, half], c_recv.at[t, col, half], dev(z, x, 1 - c)
        )

    def c_arrived(t, col, half):
        arrived((values_at, keys_at)[t][half][col].at[1 - c], c_recv.at[t, col, half])

    def spread_own(half):
        for slot in (2 * half, 2 * half + 1):
            row_arrived(1, slot)
        for ln in (2, 0, 1):
            x_copy(1, ln, half).start()
        for slot in (2 * half, 2 * half + 1):
            row_arrived(0, slot)
            values_at[half][0][c, slot - 2 * half] = v_raw[slot].reshape(2, BLK, HD)
        for ln in (2, 0, 1):
            x_copy(0, ln, half).start()
        c_copy(0, 0, half).start()

    def pass_values(half):
        for ln in (0, 1, 2):
            x_arrived(0, ln, half)
            c_copy(0, 1 + ln, half).start()

    def scaled(raw, scale, row, gain):
        scale = jnp.broadcast_to(scale[row : row + 1, :], (TOK, HD)).T
        gain = gain[pl.ds(pl.multiple_of(head * HD, HD), HD)].reshape(1, HD)
        return (raw.astype(F32) * scale * gain).astype(BF16)

    def own_scales(half):
        for i in range(2):
            slot = 2 * half + i

            @pl.when(slot != slot_mine)
            def _():
                arrived(inv_own.at[4 * part + slot], io_recv.at[4 * part + slot])

    def other_scales():
        for i in range(4):
            arrived(inv_own.at[4 - 4 * part + i], io_recv.at[4 - 4 * part + i])

    def norm_keys(col, half):
        if col > 0:
            x_arrived(1, col - 1, half)
        for i in range(2):
            slot = 2 * half + i
            if col == 0:
                scale = inv_own[4 * part + slot]
            else:
                arrived(inv_buf.at[col - 1, slot], i_recv.at[col - 1, slot])
                scale = inv_buf[col - 1, slot]
            keys = scaled(k_raw[col, slot], scale, 1, kg_in)
            keys_at[half][col][c, i] = keys.reshape(2, BLK, HD)
        c_copy(1, col, half).start()

    def norm_query(zz):
        @pl.when(zz != z)
        def _():
            arrived(q_raw.at[zz], q_recv.at[zz])

        @pl.when(zz == z)
        def _():
            own_copy(2, 0).wait()

        qbuf[zz] = scaled(q_raw[zz], inv_own[zz], 0, qg_in)

    @pl.when(active)
    def _():
        spread_own(0)
        spread_own(1)

    @pl.when(part == 0)
    def _():
        for i in range(3, 6):
            await_row(ROWS[i])
            queries_to(i)

    for yy in range(ny):

        @pl.when(yy != y)
        def _():
            arrived(sbuf.at[yy], s_recv.at[yy])

    for cp in late_loads:
        cp.wait()
    totals = sbuf[0]
    for i in range(1, ny):
        totals = totals + sbuf[i]
    inv = lax.rsqrt(totals / (NH * HD * ny) + EPS)

    isc[...] = inv

    def inv_copy(h, d):
        col = (None, 0, 2, 1)[d]
        return remote(
            isc, inv_buf.at[col, slot_mine], i_send.at[h, d], i_recv.at[col, slot_mine],
            dev(h + 4 * part, lax.rem(x + d, NX), c),
        )

    def io_copy(i):
        return remote(isc, inv_own.at[z], io_send.at[i], io_recv.at[z], dev(ROWS[i], x, c))

    inv_own[z] = inv
    for i, row in enumerate(ROWS):

        @pl.when((row != z) & (part == i // NH))
        def _():
            io_copy(i).start()

    for h in range(NH):
        for d in (2, 1, 3):
            inv_copy(h, d).start()
    for i, row in enumerate(ROWS):

        @pl.when((row != z) & (part != i // NH))
        def _():
            io_copy(i).start()

    @pl.when(part == 1)
    def _():
        for i in range(6):
            queries_to(i)

    lane = lax.broadcasted_iota(jnp.int32, (1, HD), 1)
    lane_sq = lax.broadcasted_iota(jnp.int32, (TOK, HD), 1)

    def o_copy(zz):
        return remote(
            ost.at[zz], obuf.at[head, part], o_send.at[zz], o_recv.at[head, part], dev(zz, x, c)
        )

    def t_copy(zz):
        return remote(
            stst.at[zz], stb.at[head, part], t_send.at[zz], t_recv.at[head, part], dev(zz, x, c)
        )

    def band_slot(zz, d):
        j = zz * 8 + x * 2 + c + d
        zj = jnp.clip(j, 0, 63) // 8
        ok = (zj // 4 == part) & (j >= 0) & (j <= 63)
        return lax.rem(zj, 4), jnp.where(ok, 0.0, MASKED).astype(F32)

    def second(of, col, core, slot):
        at = lax.rem(slot, 2)
        return jnp.where(slot < 2, of[0][col][core, at, 1], of[1][col][core, at, 1])

    def attend(half, pair, zz, band):
        key_parts, value_parts = [], []
        for col in (2 * pair, 2 * pair + 1):
            for core in range(NC):
                for i in range(2):
                    owner = (4 * part + 2 * half + i) * 8 + colx[col] * 2 + core
                    pick = jnp.maximum(fsm[zz, 0, owner], 0)
                    key_parts.append(keys_at[half][col][core, i, pick])
                    value_parts.append(values_at[half][col][core, i, pick])
        add = [bias[2 * half + pair, pl.ds(zz, 1), :]]
        if band:
            slot, own = band_slot(zz, 0)
            slot_two, two = band_slot(zz, 1 - 2 * c)
            slot_three, three = band_slot(zz, 2 * c - 1)
            for of, parts in ((keys_at, key_parts), (values_at, value_parts)):
                parts.append(second(of, 0, c, slot))
                parts.append(second(of, 0, 1 - c, slot_two))
                last = jnp.where(c == 0, second(of, 1, 1, slot_three), second(of, 2, 0, slot_three))
                parts += [last, last]
            add.append(jnp.where(lane < BLK, own, two))
            add.append(jnp.where(lane < BLK, three, MASKED))
        keys = jnp.concatenate(key_parts, axis=0)
        values = jnp.concatenate(value_parts, axis=0)
        scores = lax.dot_general(
            qbuf[zz], keys, (((1,), (1,)), ((), ())), preferred_element_type=F32
        ) + jnp.concatenate(add, axis=1)
        return [scores[:, i * HD : (i + 1) * HD] for i in range(scores.shape[1] // HD)], values

    def chunk(half, pair, group):
        first, last = (half, pair) == (0, 0), (half, pair) == (1, 1)
        blocks = [group * GROUP + i for i in range(GROUP)]
        scored = [attend(half, pair, zz, last) for zz in blocks]
        tops, fades, totals_of, contexts = [], [], [], []
        for zz, (tiles, _) in zip(blocks, scored):
            top = functools.reduce(jnp.maximum, tiles)
            top = jnp.broadcast_to(jnp.max(top, axis=1, keepdims=True), (TOK, HD))
            if not first:
                old = m_ref[zz]
                top = jnp.maximum(old, top)
                fades.append(jnp.exp2((old - top) * COEF))
            tops.append(top)
        for i, (zz, (tiles, values)) in enumerate(zip(blocks, scored)):
            tiles = [jnp.exp2((t - tops[i]) * COEF) for t in tiles]
            total = functools.reduce(jnp.add, tiles)
            weights = jnp.concatenate([t.astype(BF16) for t in tiles], axis=1)
            context = jnp.dot(weights, values, preferred_element_type=F32)
            if not first:
                total = l_ref[zz] * fades[i] + total
                context = acc_ref[zz] * fades[i] + context
            totals_of.append(total)
            contexts.append(context)
        if not last:
            for zz, top, total, context in zip(blocks, tops, totals_of, contexts):
                m_ref[zz] = top
                l_ref[zz] = total
                acc_ref[zz] = context
            return
        results = []
        for top, total, context in zip(tops, totals_of, contexts):
            total = jnp.broadcast_to(jnp.sum(total, axis=1, keepdims=True), (TOK, HD))
            stats = jnp.where(lane_sq == 0, top, total).T[0:8]
            results.append(((context / total).astype(BF16), stats))
        for zz, (context, stats) in zip(blocks, results):
            ost[zz] = context
            stst[zz] = stats
        for zz, (context, stats) in zip(blocks, results):

            @pl.when(zz == z)
            def _():
                obuf[head, part] = context
                stb[head, part] = stats

            @pl.when(zz != z)
            def _():
                o_copy(zz).start()
                t_copy(zz).start()

    def far_arrived(zz):
        @pl.when(zz != z)
        def _():
            arrived(fbuf.at[zz], f_recv.at[zz])

    @pl.when(active)
    def _():
        pass_values(0)

        for zz in range(NZ):
            far_arrived(zz)
        cp = pltpu.make_async_copy(fbuf, fsm, fsm_sem)
        cp.start()
        far = fbuf[:, 0, 0:64]
        block = lax.broadcasted_iota(jnp.int32, (NZ, 64), 0) * 8 + x * 2 + c
        other = lax.broadcasted_iota(jnp.int32, (NZ, 64), 1)
        valid = jnp.where((far >= 0) | (jnp.abs(block - other) <= 1), 1.0, 0.0).astype(BF16)
        at = lax.broadcasted_iota(jnp.int32, (64, 512), 1) // BLK
        src = lax.broadcasted_iota(jnp.int32, (64, 512), 0)
        for half in range(2):
            for pair in range(2):
                zsrc = 4 * part + 2 * half + lax.rem(at, 2)
                column = jnp.where(at < 4, colx[2 * pair], colx[2 * pair + 1])
                spread = (src == zsrc * 8 + column * 2 + lax.rem(at // 2, 2)).astype(F32)
                hit = jnp.dot(valid, spread.astype(BF16), preferred_element_type=F32)
                bias[2 * half + pair] = jnp.where(hit > 0.5, 0.0, MASKED)
        cp.wait()

        pass_values(1)

        def groups(group, carry):
            @pl.when((group == 0) & (part == 0))
            def _():
                own_scales(0)
                for col in range(NX):
                    norm_keys(col, 0)
                own_scales(1)

            @pl.when(group != part)
            def _():
                other_scales()

            for i in range(GROUP):
                norm_query(group * GROUP + i)

            @pl.when((group == 0) & (part == 1))
            def _():
                own_scales(0)
                for col in range(NX):
                    norm_keys(col, 0)
                own_scales(1)

            @pl.when(group == 0)
            def _():
                for col in range(NX):
                    c_arrived(0, col, 0)
                    c_arrived(0, col, 1)
                for col in range(NX):
                    norm_keys(col, 1)
                for col in range(NX):
                    c_arrived(1, col, 0)

            chunk(0, 0, group)

            chunk(0, 1, group)

            @pl.when(group == 0)
            def _():
                for col in range(NX):
                    c_arrived(1, col, 1)

            chunk(1, 0, group)
            chunk(1, 1, group)
            return carry

        lax.fori_loop(0, NZ // GROUP, groups, 0)

    start = tm * TOK
    frame = start // FRAME_TOK
    after = jnp.minimum(frame + 1, 5)
    steps = lax.broadcasted_iota(jnp.int32, gate_in.shape, 0)

    def gate_of(step):
        return jnp.sum(jnp.where(steps == step, gate_in[...], 0.0), axis=0, keepdims=True)

    gate_a, gate_b = gate_of(frame_ref[frame]), gate_of(frame_ref[after])
    edge = (frame + 1) * FRAME_TOK - start
    before = lax.broadcasted_iota(jnp.int32, (TOK, HD), 0) < edge
    for h in range(NH):
        for p in range(2):

            @pl.when(h + 4 * p != z)
            def _():
                arrived(obuf.at[h, p], o_recv.at[h, p])
                arrived(stb.at[h, p], t_recv.at[h, p])

        span = slice(h * HD, (h + 1) * HD)
        one, two = stb[h, 0], stb[h, 1]
        top = jnp.maximum(one[0:1], two[0:1])
        weight_one = one[1:2] * jnp.exp2((one[0:1] - top) * COEF)
        weight_two = two[1:2] * jnp.exp2((two[0:1] - top) * COEF)
        share = weight_one / (weight_one + weight_two)
        share = jnp.broadcast_to(share, (TOK, HD)).T
        context = obuf[h, 0].astype(F32) * share + obuf[h, 1].astype(F32) * (1.0 - share)
        gate = jnp.where(before, gate_a[:, span], gate_b[:, span])
        out_ref[:, span] = (context * gate).astype(BF16)

    for yy in range(ny):

        @pl.when(yy != y)
        def _():
            s_copy(yy).wait_send()

    for h in range(NH):
        for d in range(1, NX):
            inv_copy(h, d).wait_send()

        @pl.when(h + 4 * part != z)
        def _():
            for cp in row_copies(h):
                cp.wait_send()

    for i, row in enumerate(ROWS):

        @pl.when(row != z)
        def _():
            f_copy(i).wait_send()
            q_copy(i).wait_send()
            io_copy(i).wait_send()

    @pl.when(active)
    def _():
        for t in range(2):
            for ln in range(3):
                for half in range(2):
                    x_copy(t, ln, half).wait_send()
            for col in range(4):
                for half in range(2):
                    c_copy(t, col, half).wait_send()
        for zz in range(NZ):

            @pl.when(zz != z)
            def _():
                o_copy(zz).wait_send()
                t_copy(zz).wait_send()


def solution(mesh):
    ny = mesh.shape["head"]
    dma = pltpu.SemaphoreType.DMA
    vmem = pltpu.VMEM

    def local(query, key, value, query_gain, key_gain, gate_table, frame_step, far_blocks):
        whole = pl.BlockSpec(memory_space=pltpu.VMEM)
        hbm = pl.BlockSpec(memory_space=pltpu.HBM)
        width = NH * HD
        return pl.pallas_call(
            functools.partial(kernel, ny),
            out_shape=pltpu.VMEM((TOK, width), BF16),
            in_specs=[hbm] * 6 + [pl.BlockSpec(memory_space=pltpu.SMEM), whole],
            out_specs=whole,
            scratch_shapes=[
                vmem((TOK, width), BF16),
                vmem((TOK, width), BF16),
                vmem((width,), F32),
                vmem((width,), F32),
                vmem((50, width), F32),
                vmem((NZ, TOK, HD), BF16),
                vmem((NX, 4, TOK, HD), BF16),
                vmem((4, TOK, HD), BF16),
                vmem((8, TOK), F32),
                vmem((NZ, 8, TOK), F32),
                vmem((NX - 1, 4, 8, TOK), F32),
                vmem((NZ, TOK, HD), BF16),
                vmem((8, 128), jnp.int32),
                vmem((NZ, 8, 128), jnp.int32),
                pltpu.SMEM((NZ, 8, 128), jnp.int32),
                vmem((8, TOK), F32),
                vmem((ny, 8, TOK), F32),
                vmem((4, NZ, 512), F32),
                vmem((NZ, TOK, HD), F32),
                vmem((NZ, TOK, HD), F32),
                vmem((NZ, TOK, HD), F32),
                vmem((NZ, TOK, HD), BF16),
                vmem((NZ, 8, TOK), F32),
                vmem((NH, 2, TOK, HD), BF16),
                vmem((NH, 2, 8, TOK), F32),
                *[vmem((NC, 2, 2, BLK, HD), BF16)] * 16,
                dma((5,)), dma((3,)), dma, pltpu.SemaphoreType.REGULAR((NZ,)),
                pltpu.SemaphoreType.REGULAR((ny,)),
                dma((ny,)), dma((ny,)), dma((6,)), dma((NZ,)), dma((6,)), dma((NZ,)),
                dma((2, 3)), dma((2, 4)), dma((6,)), dma((NZ,)), dma((3, 4)), dma((3, 4)),
                dma((2, 3, 2)), dma((2, 3, 2)),
                dma((2, 4, 2)), dma((2, 4, 2)),
                dma((NZ,)), dma((NH, 2)), dma((NZ,)), dma((NH, 2)),
            ],
            compiler_params=pltpu.CompilerParams(
                collective_id=0, has_side_effects=True, vmem_limit_bytes=56 * 2**20
            ),
            name="attend",
        )(
            query, key, value, query_gain, key_gain,
            gate_table, frame_step, far_blocks,
        )

    return jax.shard_map(
        local,
        mesh=mesh,
        in_specs=(
            P("tm", "head"),
            P("tm", "head"),
            P("tm", "head"),
            P("head"),
            P("head"),
            P(None, "head"),
            P(),
            P("tm", None),
        ),
        out_specs=P("tm", "head"),
        check_vma=False,
    )
```

time: 47.8 us -> 44.5 us (0.931)
  Pallas kernels: 46 us -> 43.8 us
  local copies, waits for them, and re-layouts: 1.54 us -> 0.64 us
    pallas_call x1, Pallas kernels: 46 us -> 43.8 us  [local(): pl.pallas_call(functools.partial(kernel, ny), out_shape=pltpu.VMEM((TOK,...]
    unnamed x1, local copies, waits for them, and re-layouts: 1.54 us -> 0.64 us
where the time goes in v2:
time: 44.5 us; the launch traced here: 44.4 us
  Pallas kernels  43.8 us (98%)
  local copies, waits for them, and re-layouts  0.64 us (1%)
    pallas_call x1, Pallas kernels, local(): pl.pallas_call(functools.partial(kernel, ny), out_shape=pltpu.VMEM((TOK,...  43.8 us

profile of v2, /device:TPU:1, one launch (start us, length us, event | category | flops | bytes accessed | tf_op | source)
XLA Modules:
  0.0 44.4 jit_solution(15696710340867751204)
XLA Ops:
  0.0 43.8 %attend.1 = bf16[128,384]{1,0:T(8,128)(2,1)S(1)} custom-call(bf16[128,384]{1,0:T(8,128)(2,1)} %q_hbm.1, bf16[128,384]{1,0:T(8,128)(2,1)} %k_hbm.1, bf16[128,384]{1,0:T(8,128)(2,1)} %v_hbm.1, f32[384]{0:T(512)} %qg_hbm.1, f32[384]{0:T(512)} %kg_hbm.1, f32[50,384]{1,0:T(8,128)} %gate_hbm.1, s32[6]{0:T(128)} %frame_ref.1, s32[1,64]{1,0:T(1,128)} %far_ref.1), custom_call_target="tpu_custom_call" | custom-call | tf_op jit(solution)/shard_map/attend/pallas_call | solution.py:615
  43.8 0.6 %copy.10 = bf16[128,384]{1,0:T(8,128)(2,1)} copy(bf16[128,384]{1,0:T(8,128)(2,1)S(1)} %attend.1) | data formatting | bytes 196608

commit v3 on v2

--- a/solution.py
+++ b/solution.py
@@ -19,6 +19,7 @@
 LOG2E = 1.4426950408889634
 COEF = HD**-0.5 * LOG2E
 MESH = pl.DeviceIdType.MESH
+TWO = pl.ds(0, 2)
 BF16 = jnp.bfloat16
 F32 = jnp.float32
 
@@ -121,8 +122,9 @@
             remote(
                 ref.at[:, cols], dst, p1_send.at[t, h], p1_recv.at[t, slot_mine], dev(row, x, c)
             )
-            for t, (ref, dst) in enumerate(
-                ((v_hbm, v_raw.at[slot_mine]), (k_hbm, k_raw.at[0, slot_mine]))
+            for t, ref, dst in (
+                (1, k_hbm, k_raw.at[0, slot_mine]),
+                (0, v_hbm, v_raw.at[slot_mine]),
             )
         ]
 
@@ -139,32 +141,37 @@
         source = q_hbm.at[:, pl.ds(i % NH * HD, HD)]
         return remote(source, q_raw.at[z], q_send.at[i], q_recv.at[z], dev(ROWS[i], x, c))
 
+    def far_to(i):
+        @pl.when(ROWS[i] != z)
+        def _():
+            f_copy(i).start()
+
     def queries_to(i):
         @pl.when(ROWS[i] != z)
         def _():
-            f_copy(i).start()
             q_copy(i).start()
 
     far_row = jnp.concatenate([far_ref[...], jnp.full((1, 64), -1, jnp.int32)], axis=1)
     fst[...] = jnp.broadcast_to(far_row, (8, 128))
     fbuf[z] = fst[...]
-    for p in range(2):
-
-        @pl.when(part == p)
-        def _():
-            for h in range(NH):
-                row = h + 4 * p
-                await_row(row)
-
-                @pl.when(row != z)
-                def _():
-                    for cp in row_copies(h):
-                        cp.start()
-
-                @pl.when(row == z)
-                def _():
-                    for t in range(3):
-                        own_copy(t, h).start()
+    def keys_to(i):
+        row = ROWS[i]
+
+        @pl.when(row != z)
+        def _():
+            for cp in row_copies(i % NH):
+                cp.start()
+
+        @pl.when(row == z)
+        def _():
+            for t in range(3):
+                own_copy(t, i % NH).start()
+
+    for i in range(6):
+
+        @pl.when((part == i // NH) & (ROWS[i] <= z))
+        def _():
+            keys_to(i)
 
     for cp in loads:
         cp.wait()
@@ -181,13 +188,27 @@
     sbuf[y] = sst[...]
 
     def s_copy(yy):
-        return remote(sst, sbuf.at[y], s_send.at[yy], s_recv.at[y], (tm, yy))
+        return remote(sst.at[TWO], sbuf.at[y, TWO], s_send.at[yy], s_recv.at[y], (tm, yy))
 
     for yy in range(ny - 1):
 
         @pl.when(yy < y)
         def _():
             s_copy(yy).start()
+
+    for i in range(6):
+
+        @pl.when((part == i // NH) & (ROWS[i] > z))
+        def _():
+            await_row(ROWS[i])
+            keys_to(i)
+
+    for p in range(2):
+
+        @pl.when(part == p)
+        def _():
+            for i in range(3 + 3 * p):
+                far_to(i)
 
     @pl.when(part == 0)
     def _():
@@ -268,11 +289,11 @@
 
             @pl.when(slot != slot_mine)
             def _():
-                arrived(inv_own.at[4 * part + slot], io_recv.at[4 * part + slot])
+                arrived(inv_own.at[4 * part + slot, TWO], io_recv.at[4 * part + slot])
 
     def other_scales():
         for i in range(4):
-            arrived(inv_own.at[4 - 4 * part + i], io_recv.at[4 - 4 * part + i])
+            arrived(inv_own.at[4 - 4 * part + i, TWO], io_recv.at[4 - 4 * part + i])
 
     def norm_keys(col, half):
         if col > 0:
@@ -282,7 +303,7 @@
             if col == 0:
                 scale = inv_own[4 * part + slot]
             else:
-                arrived(inv_buf.at[col - 1, slot], i_recv.at[col - 1, slot])
+                arrived(inv_buf.at[col - 1, slot, TWO], i_recv.at[col - 1, slot])
                 scale = inv_buf[col - 1, slot]
             keys = scaled(k_raw[col, slot], scale, 1, kg_in)
             keys_at[half][col][c, i] = keys.reshape(2, BLK, HD)
@@ -304,17 +325,23 @@
         spread_own(0)
         spread_own(1)
 
+    @pl.when(part == 1)
+    def _():
+        for i in range(6):
+            queries_to(i)
+
     @pl.when(part == 0)
     def _():
         for i in range(3, 6):
             await_row(ROWS[i])
+            far_to(i)
             queries_to(i)
 
     for yy in range(ny):
 
         @pl.when(yy != y)
         def _():
-            arrived(sbuf.at[yy], s_recv.at[yy])
+            arrived(sbuf.at[yy, TWO], s_recv.at[yy])
 
     for cp in late_loads:
         cp.wait()
@@ -328,12 +355,14 @@
     def inv_copy(h, d):
         col = (None, 0, 2, 1)[d]
         return remote(
-            isc, inv_buf.at[col, slot_mine], i_send.at[h, d], i_recv.at[col, slot_mine],
+            isc.at[TWO], inv_buf.at[col, slot_mine, TWO], i_send.at[h, d], i_recv.at[col, slot_mine],
             dev(h + 4 * part, lax.rem(x + d, NX), c),
         )
 
     def io_copy(i):
-        return remote(isc, inv_own.at[z], io_send.at[i], io_recv.at[z], dev(ROWS[i], x, c))
+        return remote(
+            isc.at[TWO], inv_own.at[z, TWO], io_send.at[i], io_recv.at[z], dev(ROWS[i], x, c)
+        )
 
     inv_own[z] = inv
     for i, row in enumerate(ROWS):
@@ -351,11 +380,6 @@
         def _():
             io_copy(i).start()
 
-    @pl.when(part == 1)
-    def _():
-        for i in range(6):
-            queries_to(i)
-
     lane = lax.broadcasted_iota(jnp.int32, (1, HD), 1)
     lane_sq = lax.broadcasted_iota(jnp.int32, (TOK, HD), 1)
 
@@ -366,7 +390,7 @@
 
     def t_copy(zz):
         return remote(
-            stst.at[zz], stb.at[head, part], t_send.at[zz], t_recv.at[head, part], dev(zz, x, c)
+            stst.at[zz, TWO], stb.at[head, part, TWO], t_send.at[zz], t_recv.at[head, part], dev(zz, x, c)
         )
 
     def band_slot(zz, d):
@@ -484,47 +508,49 @@
                 bias[2 * half + pair] = jnp.where(hit > 0.5, 0.0, MASKED)
         cp.wait()
 
-        pass_values(1)
-
         def groups(group, carry):
             @pl.when((group == 0) & (part == 0))
             def _():
                 own_scales(0)
+                own_scales(1)
+
+            @pl.when(group != part)
+            def _():
+                other_scales()
+
+            for i in range(GROUP):
+                norm_query(group * GROUP + i)
+
+            @pl.when((group == 0) & (part == 1))
+            def _():
+                own_scales(0)
+
+            @pl.when(group == 0)
+            def _():
                 for col in range(NX):
                     norm_keys(col, 0)
-                own_scales(1)
-
-            @pl.when(group != part)
-            def _():
-                other_scales()
-
-            for i in range(GROUP):
-                norm_query(group * GROUP + i)
-
-            @pl.when((group == 0) & (part == 1))
-            def _():
-                own_scales(0)
-                for col in range(NX):
-                    norm_keys(col, 0)
-                own_scales(1)
-
-            @pl.when(group == 0)
-            def _():
                 for col in range(NX):
                     c_arrived(0, col, 0)
-                    c_arrived(0, col, 1)
+                    c_arrived(1, col, 0)
+
+            chunk(0, 0, group)
+
+            @pl.when((group == 0) & (part == 1))
+            def _():
+                own_scales(1)
+
+            @pl.when(group == 0)
+            def _():
                 for col in range(NX):
                     norm_keys(col, 1)
+                pass_values(1)
+
+            chunk(0, 1, group)
+
+            @pl.when(group == 0)
+            def _():
                 for col in range(NX):
-                    c_arrived(1, col, 0)
-
-            chunk(0, 0, group)
-
-            chunk(0, 1, group)
-
-            @pl.when(group == 0)
-            def _():
-                for col in range(NX):
+                    c_arrived(0, col, 1)
                     c_arrived(1, col, 1)
 
             chunk(1, 0, group)
@@ -550,7 +576,7 @@
             @pl.when(h + 4 * p != z)
             def _():
                 arrived(obuf.at[h, p], o_recv.at[h, p])
-                arrived(stb.at[h, p], t_recv.at[h, p])
+                arrived(stb.at[h, p, TWO], t_recv.at[h, p])
 
         span = slice(h * HD, (h + 1) * HD)
         one, two = stb[h, 0], stb[h, 1]

time: 44.5 us -> 43.6 us (0.980); the launches traced: 44.4 us -> 42.8 us
  Pallas kernels: 43.8 us -> 42.1 us
    pallas_call x1, Pallas kernels: 43.8 us -> 42.1 us  [local(): pl.pallas_call(functools.partial(kernel, ny), out_shape=pltpu.VMEM((TOK,...]
where the time goes in v3:
time: 43.6 us; the launch traced here: 42.8 us
  Pallas kernels  42.1 us (97%)
  local copies, waits for them, and re-layouts  0.64 us (1%)
    pallas_call x1, Pallas kernels, local(): pl.pallas_call(functools.partial(kernel, ny), out_shape=pltpu.VMEM((TOK,...  42.1 us

profile of v3, /device:TPU:1, one launch (start us, length us, event | category | flops | bytes accessed | tf_op | source)
XLA Modules:
  0.0 42.8 jit_solution(4274029922159705038)
XLA Ops:
  0.0 42.1 %attend.1 = bf16[128,384]{1,0:T(8,128)(2,1)S(1)} custom-call(bf16[128,384]{1,0:T(8,128)(2,1)} %q_hbm.1, bf16[128,384]{1,0:T(8,128)(2,1)} %k_hbm.1, bf16[128,384]{1,0:T(8,128)(2,1)} %v_hbm.1, f32[384]{0:T(512)} %qg_hbm.1, f32[384]{0:T(512)} %kg_hbm.1, f32[50,384]{1,0:T(8,128)} %gate_hbm.1, s32[6]{0:T(128)} %frame_ref.1, s32[1,64]{1,0:T(1,128)} %far_ref.1), custom_call_target="tpu_custom_call" | custom-call | tf_op jit(solution)/shard_map/attend/pallas_call | solution.py:641
  42.1 0.6 %copy.10 = bf16[128,384]{1,0:T(8,128)(2,1)} copy(bf16[128,384]{1,0:T(8,128)(2,1)S(1)} %attend.1) | data formatting | bytes 196608

commit v4 on v3

--- a/solution.py
+++ b/solution.py
@@ -154,24 +154,29 @@
     far_row = jnp.concatenate([far_ref[...], jnp.full((1, 64), -1, jnp.int32)], axis=1)
     fst[...] = jnp.broadcast_to(far_row, (8, 128))
     fbuf[z] = fst[...]
-    def keys_to(i):
+    def keys_to(i, t):
         row = ROWS[i]
 
         @pl.when(row != z)
         def _():
-            for cp in row_copies(i % NH):
-                cp.start()
+            row_copies(i % NH)[1 - t].start()
 
         @pl.when(row == z)
         def _():
-            for t in range(3):
-                own_copy(t, i % NH).start()
-
-    for i in range(6):
-
-        @pl.when((part == i // NH) & (ROWS[i] <= z))
-        def _():
-            keys_to(i)
+            own_copy(t, i % NH).start()
+
+    for i, row in enumerate(ROWS):
+
+        @pl.when(row == z)
+        def _():
+            own_copy(2, i % NH).start()
+
+    for t in (1, 0):
+        for i in range(6):
+
+            @pl.when((part == i // NH) & (ROWS[i] <= z))
+            def _():
+                keys_to(i, t)
 
     for cp in loads:
         cp.wait()
@@ -201,7 +206,8 @@
         @pl.when((part == i // NH) & (ROWS[i] > z))
         def _():
             await_row(ROWS[i])
-            keys_to(i)
+            keys_to(i, 1)
+            keys_to(i, 0)
 
     for p in range(2):
 
@@ -559,6 +565,39 @@
 
         lax.fori_loop(0, NZ // GROUP, groups, 0)
 
+    for yy in range(ny):
+
+        @pl.when(yy != y)
+        def _():
+            s_copy(yy).wait_send()
+
+    for h in range(NH):
+        for d in range(1, NX):
+            inv_copy(h, d).wait_send()
+
+        @pl.when(h + 4 * part != z)
+        def _():
+            for cp in row_copies(h):
+                cp.wait_send()
+
+    for i, row in enumerate(ROWS):
+
+        @pl.when(row != z)
+        def _():
+            f_copy(i).wait_send()
+            q_copy(i).wait_send()
+            io_copy(i).wait_send()
+
+    @pl.when(active)
+    def _():
+        for t in range(2):
+            for ln in range(3):
+                for half in range(2):
+                    x_copy(t, ln, half).wait_send()
+            for col in range(4):
+                for half in range(2):
+                    c_copy(t, col, half).wait_send()
+
     start = tm * TOK
     frame = start // FRAME_TOK
     after = jnp.minimum(frame + 1, 5)
@@ -589,38 +628,8 @@
         gate = jnp.where(before, gate_a[:, span], gate_b[:, span])
         out_ref[:, span] = (context * gate).astype(BF16)
 
-    for yy in range(ny):
-
-        @pl.when(yy != y)
-        def _():
-            s_copy(yy).wait_send()
-
-    for h in range(NH):
-        for d in range(1, NX):
-            inv_copy(h, d).wait_send()
-
-        @pl.when(h + 4 * part != z)
-        def _():
-            for cp in row_copies(h):
-                cp.wait_send()
-
-    for i, row in enumerate(ROWS):
-
-        @pl.when(row != z)
-        def _():
-            f_copy(i).wait_send()
-            q_copy(i).wait_send()
-            io_copy(i).wait_send()
-
     @pl.when(active)
     def _():
-        for t in range(2):
-            for ln in range(3):
-                for half in range(2):
-                    x_copy(t, ln, half).wait_send()
-            for col in range(4):
-                for half in range(2):
-                    c_copy(t, col, half).wait_send()
         for zz in range(NZ):
 
             @pl.when(zz != z)

time: 43.6 us -> 43.5 us (level)
  no operation moved by 1% of the time
where the time goes in v4:
time: 43.5 us; the launch traced here: 42.7 us
  Pallas kernels  42 us (97%)
  local copies, waits for them, and re-layouts  0.64 us (1%)
    pallas_call x1, Pallas kernels, local(): pl.pallas_call(functools.partial(kernel, ny), out_shape=pltpu.VMEM((TOK,...  42 us

profile of v4, /device:TPU:1, one launch (start us, length us, event | category | flops | bytes accessed | tf_op | source)
XLA Modules:
  0.0 42.7 jit_solution(499690649879781876)
XLA Ops:
  0.0 42.0 %attend.1 = bf16[128,384]{1,0:T(8,128)(2,1)S(1)} custom-call(bf16[128,384]{1,0:T(8,128)(2,1)} %q_hbm.1, bf16[128,384]{1,0:T(8,128)(2,1)} %k_hbm.1, bf16[128,384]{1,0:T(8,128)(2,1)} %v_hbm.1, f32[384]{0:T(512)} %qg_hbm.1, f32[384]{0:T(512)} %kg_hbm.1, f32[50,384]{1,0:T(8,128)} %gate_hbm.1, s32[6]{0:T(128)} %frame_ref.1, s32[1,64]{1,0:T(1,128)} %far_ref.1), custom_call_target="tpu_custom_call" | custom-call | tf_op jit(solution)/shard_map/attend/pallas_call | solution.py:650
  42.0 0.6 %copy.10 = bf16[128,384]{1,0:T(8,128)(2,1)} copy(bf16[128,384]{1,0:T(8,128)(2,1)S(1)} %attend.1) | data formatting | bytes 196608
